TPU v7x, 32 devices: a whole 2x2x4 slice. The times are simulated.
32 devices in a mesh: dp: 8 (over z, y), head: 4 (over x, core).
Axes of the slice: x: 2, y: 2, z: 4, core: 2. Of those that a mesh axis runs over, the one named last changes fastest.
Arguments:
- decoder_in: bfloat16 [8192, 768], P(('dp', 'head')), may hold values from -6 to 6
- encoder_out: bfloat16 [32, 1024, 768], P('dp', 'head'), may hold values from -6 to 6
- encoder_segment: int32 [32, 1024], P('dp'), may hold values from 0 to 15, never falling along the last dimension, each value on 1 to 512 neighbouring positions
- slot_segment: int32 [32, 16], P('dp'), may hold values from 0 to 15, each once within a row
- position_bucket: int32 [16, 16], replicated, may hold values from 0 to 31
- self_gain: float32 [768], replicated, may hold values from 0.5 to 1.5
- self_query: bfloat16 [768, 768], replicated, may hold values from -0.4375 to 0.4375
- self_key: bfloat16 [768, 768], replicated, may hold values from -0.21875 to 0.21875
- self_value: bfloat16 [768, 768], replicated, may hold values from -0.21875 to 0.21875
- self_output: bfloat16 [768, 768], replicated, may hold values from -0.4375 to 0.4375
- position_bias: float32 [32, 12], replicated, may hold values from -4 to 4
- cross_gain: float32 [768], replicated, may hold values from 0.5 to 1.5
- cross_query: bfloat16 [768, 768], replicated, may hold values from -0.4375 to 0.4375
- cross_key: bfloat16 [768, 768], replicated, may hold values from -0.21875 to 0.21875
- cross_value: bfloat16 [768, 768], replicated, may hold values from -0.21875 to 0.21875
- cross_output: bfloat16 [768, 768], replicated, may hold values from -0.875 to 0.875
- feed_gain: float32 [768], replicated, may hold values from 0.5 to 1.5
- feed_in: bfloat16 [768, 3072], replicated, may hold values from -0.21875 to 0.21875
- feed_out: bfloat16 [3072, 768], replicated, may hold values from -0.15625 to 0.15625
- score_row: bfloat16 [768], replicated, may hold values from -6 to 6
- grad_hidden: float32 [8192, 768], P(('dp', 'head')), may hold values from -6 to 6
- grad_score: float32 [8192], P(('dp', 'head')), may hold values from -6 to 6
Outputs:
- hidden_out: bfloat16 [8192, 768], P(('dp', 'head'))
- ranking_score: float32 [8192], P(('dp', 'head'))
- decoder_grad: float32 [8192, 768], P(('dp', 'head'))
- encoder_grad: float32 [32, 1024, 768], P('dp', 'head')
- self_gain_grad: float32 [768], P('head')
- self_query_grad: float32 [768, 768], P('head')
- self_key_grad: float32 [768, 768], P('head')
- self_value_grad: float32 [768, 768], P('head')
- self_output_grad: float32 [768, 768], P('head')
- position_bias_grad: float32 [32, 12], P('head')
- cross_gain_grad: float32 [768], P('head')
- cross_query_grad: float32 [768, 768], P('head')
- cross_key_grad: float32 [768, 768], P('head')
- cross_value_grad: float32 [768, 768], P('head')
- cross_output_grad: float32 [768, 768], P('head')
- feed_gain_grad: float32 [768], P('head')
- feed_in_grad: float32 [768, 3072], P('head')
- feed_out_grad: float32 [3072, 768], P('head')
- score_row_grad: float32 [768], P('head')
Inputs may be any that keep to these rules, and one draw needn't show every extreme that they name: `encoder_segment`: in every row the numbers never fall along the 1024 positions, each of 0 to 15 occurs, no segment holds more than 512 positions and some segment holds exactly that many. `slot_segment`: each row's 16 slots name each of that row's segments once.
All inputs are finite; a program needn't handle non-finite values.
Results may differ from a plain program's by a relative error of at most 0.022.
The roundings to bfloat16 on the way count: a program that leaves them out, or rounds other values in their place, can miss the bound.
Values may be sent and summed in bfloat16 or wider, within the bound.
No kernel may reach another device: no remote copies, remote signals or barrier semaphores. Data moves between devices by JAX's collectives and lax.ppermute only.
A program may use at most 192 MiB of HBM per device.

v0:
```python
import jax
import jax.numpy as jnp
from jax import lax
from jax.sharding import PartitionSpec as P

EPSILON = 1e-06
MASKED = -1e30
PRECISE = lax.Precision.HIGHEST


def rms_norm(hidden, norm_gain):
    return (
        hidden * lax.rsqrt(jnp.mean(hidden * hidden, axis=-1, keepdims=True) + EPSILON) * norm_gain
    )


def norm_back(hidden, norm_gain, upstream):
    normed, pullback = jax.vjp(rms_norm, hidden, norm_gain)
    return pullback(upstream)


def gelu_curve(values):
    return jax.nn.gelu(values, approximate=True)


def matmul(first_factor, second_factor):
    return jnp.dot(first_factor, second_factor, preferred_element_type=jnp.float32)


def contract_rows(first_factor, second_factor):
    return lax.dot_general(
        first_factor, second_factor, (((0,), (0,)), ((), ())), preferred_element_type=jnp.float32
    )


def contract_cols(first_factor, second_factor):
    return lax.dot_general(
        first_factor, second_factor, (((1,), (1,)), ((), ())), preferred_element_type=jnp.float32
    )


def block_rows(row_count, per_row):
    target = max(1, -(-512 // per_row))
    chosen = row_count
    for option in range(row_count, 0, -1):
        if row_count % option == 0 and option >= target:
            chosen = option
    return chosen


def by_blocks(function, arrays, rows_each):
    row_total = arrays[0].shape[0]
    block_count = row_total // rows_each
    shaped = tuple(
        (member.reshape((block_count, rows_each) + member.shape[1:]) for member in arrays)
    )
    results = lax.map(lambda members: function(*members), shaped)
    return jax.tree.map(lambda member: member.reshape((row_total,) + member.shape[2:]), results)


def masked_scores(query_heads, key_heads, query_segment, key_segment):
    products = jnp.einsum(
        "rqhd,rkhd->rhqk", query_heads, key_heads, preferred_element_type=jnp.float32
    )
    allowed = query_segment[:, None, :, None] == key_segment[:, None, None, :]
    return (jnp.where(allowed, products * query_heads.shape[-1] ** (-0.5), MASKED), allowed)


def attend_whole(query_heads, key_heads, value_heads, query_segment, key_segment):
    scores, allowed = masked_scores(query_heads, key_heads, query_segment, key_segment)
    highest = jnp.max(scores, axis=-1)
    masses = jnp.sum(jnp.where(allowed, jnp.exp(scores - highest[..., None]), 0.0), axis=-1)
    log_totals = highest + jnp.log(masses)
    weights = jnp.where(allowed, jnp.exp(scores - log_totals[..., None]), 0.0).astype(jnp.bfloat16)
    outputs = jnp.einsum(
        "rhqk,rkhd->rqhd", weights, value_heads, preferred_element_type=jnp.float32
    )
    return (outputs, log_totals)


def softmax_pieces(
    query_heads, key_heads, value_heads, grad_heads, query_segment, key_segment, log_totals
):
    scores, allowed = masked_scores(query_heads, key_heads, query_segment, key_segment)
    weights = jnp.where(allowed, jnp.exp(scores - log_totals[..., None]), 0.0)
    grad_weights = jnp.einsum(
        "rqhd,rkhd->rhqk", grad_heads, value_heads, preferred_element_type=jnp.float32
    )
    return (weights, grad_weights)


def finish_grads(query_heads, key_heads, grad_heads, weights, grad_weights, dot_sums):
    grad_scores = (weights * (grad_weights - dot_sums[..., None])).astype(jnp.bfloat16)
    score_scale = query_heads.shape[-1] ** (-0.5)
    grad_query = (
        jnp.einsum("rhqk,rkhd->rqhd", grad_scores, key_heads, preferred_element_type=jnp.float32)
        * score_scale
    )
    grad_key = (
        jnp.einsum("rhqk,rqhd->rkhd", grad_scores, query_heads, preferred_element_type=jnp.float32)
        * score_scale
    )
    grad_value = jnp.einsum(
        "rhqk,rqhd->rkhd",
        weights.astype(jnp.bfloat16),
        grad_heads,
        preferred_element_type=jnp.float32,
    )
    return (grad_query, grad_key, grad_value)


def local_grads(
    query_heads, key_heads, value_heads, grad_heads, query_segment, key_segment, log_totals
):
    weights, grad_weights = softmax_pieces(
        query_heads, key_heads, value_heads, grad_heads, query_segment, key_segment, log_totals
    )
    return finish_grads(
        query_heads,
        key_heads,
        grad_heads,
        weights,
        grad_weights,
        jnp.sum(weights * grad_weights, axis=-1),
    )


def body(
    decoder_in,
    encoder_out,
    encoder_segment,
    slot_segment,
    position_bucket,
    self_gain,
    self_query,
    self_key,
    self_value,
    self_output,
    position_bias,
    cross_gain,
    cross_query,
    cross_key,
    cross_value,
    cross_output,
    feed_gain,
    feed_in,
    feed_out,
    score_row,
    grad_hidden,
    grad_score,
):
    tokens = decoder_in.astype(jnp.float32)
    tok_count = tokens.shape[0]
    model_width = tokens.shape[1]
    bucket_count = position_bias.shape[0]
    head_count = position_bias.shape[1]
    head_width = model_width // head_count
    step_count = position_bucket.shape[0]
    slot_count = tok_count // step_count
    group_size = lax.axis_size("head")
    row_count = encoder_out.shape[0]
    part_len = encoder_out.shape[1]
    pair_count = slot_segment.shape[1]
    per_row = pair_count * step_count
    rows_each = block_rows(row_count, per_row)
    score_scale = head_width ** (-0.5)

    def slot_heads(matrix):
        return matrix.reshape(slot_count, step_count, head_count, head_width)

    act_one = rms_norm(tokens, self_gain).astype(jnp.bfloat16)
    query_one = slot_heads(matmul(act_one, self_query).astype(jnp.bfloat16))
    key_one = slot_heads(matmul(act_one, self_key).astype(jnp.bfloat16))
    value_one = slot_heads(matmul(act_one, self_value).astype(jnp.bfloat16))
    onehot = (
        position_bucket[:, :, None] == jnp.arange(bucket_count, dtype=jnp.int32)[None, None, :]
    ).astype(jnp.float32)
    bias_table = jnp.einsum("ijb,bh->hij", onehot, position_bias, precision=PRECISE)
    products_one = jnp.einsum(
        "nihd,njhd->nhij", query_one, key_one, preferred_element_type=jnp.float32
    )
    causal = jnp.arange(step_count)[:, None] >= jnp.arange(step_count)[None, :]
    scores_one = jnp.where(causal, products_one * score_scale + bias_table[None], MASKED)
    shifted = jnp.exp(scores_one - jnp.max(scores_one, axis=-1, keepdims=True))
    attention_one = shifted / jnp.sum(shifted, axis=-1, keepdims=True)
    weights_one = attention_one.astype(jnp.bfloat16)
    mixed_one = jnp.einsum(
        "nhij,njhd->nihd", weights_one, value_one, preferred_element_type=jnp.float32
    )
    mixed_one = mixed_one.reshape(tok_count, model_width).astype(jnp.bfloat16)
    residual_one = tokens + matmul(mixed_one, self_output)
    act_two = rms_norm(residual_one, cross_gain).astype(jnp.bfloat16)
    query_two = matmul(act_two, cross_query).astype(jnp.bfloat16)
    encoder_rows = encoder_out.reshape(row_count * part_len, model_width)
    key_two = (
        matmul(encoder_rows, cross_key)
        .astype(jnp.bfloat16)
        .reshape(row_count, part_len, model_width)
    )
    value_two = (
        matmul(encoder_rows, cross_value)
        .astype(jnp.bfloat16)
        .reshape(row_count, part_len, model_width)
    )
    query_segment = jnp.repeat(slot_segment, step_count, axis=1)
    group_query = lax.all_to_all(query_two, "head", split_axis=1, concat_axis=0, tiled=True)
    group_key, group_value = (
        lax.all_to_all(key_two, "head", split_axis=2, concat_axis=1, tiled=True),
        lax.all_to_all(value_two, "head", split_axis=2, concat_axis=1, tiled=True),
    )
    local_heads = head_count // group_size
    key_len = group_key.shape[1]
    query_heads = group_query.reshape(row_count, per_row, local_heads, head_width)
    key_heads = group_key.reshape(row_count, key_len, local_heads, head_width)
    value_heads = group_value.reshape(row_count, key_len, local_heads, head_width)
    outputs, log_totals = by_blocks(
        attend_whole,
        (query_heads, key_heads, value_heads, query_segment, encoder_segment),
        rows_each,
    )
    outputs = outputs.astype(jnp.bfloat16).reshape(group_size * tok_count, local_heads * head_width)
    mixed_two = lax.all_to_all(outputs, "head", split_axis=0, concat_axis=1, tiled=True)
    residual_two = residual_one + matmul(mixed_two, cross_output)
    act_three = rms_norm(residual_two, feed_gain).astype(jnp.bfloat16)
    pre_act = matmul(act_three, feed_in)
    hidden_full, gelu_back = jax.vjp(gelu_curve, pre_act)
    hidden_low = hidden_full.astype(jnp.bfloat16)
    residual_three = residual_two + matmul(hidden_low, feed_out)
    row_float = score_row.astype(jnp.float32)
    ranking_score = jnp.sum(residual_three * row_float, axis=-1) * model_width ** (-0.5)
    scaled_grad = grad_score * model_width ** (-0.5)
    upstream = grad_hidden + scaled_grad[:, None] * row_float
    grad_row = jnp.sum(scaled_grad[:, None] * residual_three, axis=0)
    upstream_low = upstream.astype(jnp.bfloat16)
    grad_feed_out = contract_rows(hidden_low, upstream_low)
    grad_pre = gelu_back(contract_cols(upstream_low, feed_out))[0].astype(jnp.bfloat16)
    grad_feed_in = contract_rows(act_three, grad_pre)
    grad_norm_three, grad_feed_gain = norm_back(
        residual_two, feed_gain, contract_cols(grad_pre, feed_in)
    )
    grad_two = upstream + grad_norm_three
    grad_two_low = grad_two.astype(jnp.bfloat16)
    grad_cross_output = contract_rows(mixed_two, grad_two_low)
    grad_mixed = contract_cols(grad_two_low, cross_output).astype(jnp.bfloat16)
    group_grad = lax.all_to_all(grad_mixed, "head", split_axis=1, concat_axis=0, tiled=True)
    grad_heads = group_grad.reshape(row_count, per_row, local_heads, head_width)
    grad_query, grad_key, grad_value = by_blocks(
        local_grads,
        (
            query_heads,
            key_heads,
            value_heads,
            grad_heads,
            query_segment,
            encoder_segment,
            log_totals,
        ),
        rows_each,
    )
    query_back = lax.all_to_all(
        grad_query.astype(jnp.bfloat16).reshape(group_size * tok_count, local_heads * head_width),
        "head",
        split_axis=0,
        concat_axis=1,
        tiled=True,
    )
    key_back, value_back = (
        lax.all_to_all(
            grad_key.astype(jnp.bfloat16).reshape(row_count, key_len, local_heads * head_width),
            "head",
            split_axis=1,
            concat_axis=2,
            tiled=True,
        ),
        lax.all_to_all(
            grad_value.astype(jnp.bfloat16).reshape(row_count, key_len, local_heads * head_width),
            "head",
            split_axis=1,
            concat_axis=2,
            tiled=True,
        ),
    )
    grad_cross_query = contract_rows(act_two, query_back)
    key_flat = key_back.reshape(row_count * part_len, model_width)
    value_flat = value_back.reshape(row_count * part_len, model_width)
    grad_cross_key = contract_rows(encoder_rows, key_flat)
    grad_cross_value = contract_rows(encoder_rows, value_flat)
    grad_encoder = (
        contract_cols(key_flat, cross_key) + contract_cols(value_flat, cross_value)
    ).reshape(row_count, part_len, model_width)
    grad_norm_two, grad_cross_gain = norm_back(
        residual_one, cross_gain, contract_cols(query_back, cross_query)
    )
    grad_one = grad_two + grad_norm_two
    grad_one_low = grad_one.astype(jnp.bfloat16)
    grad_self_output = contract_rows(mixed_one, grad_one_low)
    grad_mixed_one = slot_heads(contract_cols(grad_one_low, self_output).astype(jnp.bfloat16))
    grad_weights_one = jnp.einsum(
        "nihd,njhd->nhij", grad_mixed_one, value_one, preferred_element_type=jnp.float32
    )
    dots_one = jnp.sum(attention_one * grad_weights_one, axis=-1, keepdims=True)
    grad_scores_one = (attention_one * (grad_weights_one - dots_one)).astype(jnp.bfloat16)
    grad_bias = jnp.einsum(
        "nhij,ijb->bh", grad_scores_one.astype(jnp.float32), onehot, precision=PRECISE
    )
    query_grad_one = (
        (
            jnp.einsum(
                "nhij,njhd->nihd", grad_scores_one, key_one, preferred_element_type=jnp.float32
            )
            * score_scale
        )
        .astype(jnp.bfloat16)
        .reshape(tok_count, model_width)
    )
    key_grad_one = (
        (
            jnp.einsum(
                "nhij,nihd->njhd", grad_scores_one, query_one, preferred_element_type=jnp.float32
            )
            * score_scale
        )
        .astype(jnp.bfloat16)
        .reshape(tok_count, model_width)
    )
    value_grad_one = (
        jnp.einsum(
            "nhij,nihd->njhd", weights_one, grad_mixed_one, preferred_element_type=jnp.float32
        )
        .astype(jnp.bfloat16)
        .reshape(tok_count, model_width)
    )
    grad_self_query = contract_rows(act_one, query_grad_one)
    grad_self_key = contract_rows(act_one, key_grad_one)
    grad_self_value = contract_rows(act_one, value_grad_one)
    upstream_one = (
        contract_cols(query_grad_one, self_query)
        + contract_cols(key_grad_one, self_key)
        + contract_cols(value_grad_one, self_value)
    )
    grad_norm_one, grad_self_gain = norm_back(tokens, self_gain, upstream_one)
    grad_input = grad_one + grad_norm_one
    shards = (
        lax.psum_scatter(
            grad_self_gain.astype(jnp.bfloat16), "head", scatter_dimension=0, tiled=True
        ).astype(jnp.float32),
        lax.psum_scatter(
            grad_self_query.astype(jnp.bfloat16), "head", scatter_dimension=0, tiled=True
        ).astype(jnp.float32),
        lax.psum_scatter(
            grad_self_key.astype(jnp.bfloat16), "head", scatter_dimension=0, tiled=True
        ).astype(jnp.float32),
        lax.psum_scatter(
            grad_self_value.astype(jnp.bfloat16), "head", scatter_dimension=0, tiled=True
        ).astype(jnp.float32),
        lax.psum_scatter(
            grad_self_output.astype(jnp.bfloat16), "head", scatter_dimension=0, tiled=True
        ).astype(jnp.float32),
        lax.psum_scatter(
            grad_bias.astype(jnp.bfloat16), "head", scatter_dimension=0, tiled=True
        ).astype(jnp.float32),
        lax.psum_scatter(
            grad_cross_gain.astype(jnp.bfloat16), "head", scatter_dimension=0, tiled=True
        ).astype(jnp.float32),
        lax.psum_scatter(
            grad_cross_query.astype(jnp.bfloat16), "head", scatter_dimension=0, tiled=True
        ).astype(jnp.float32),
        lax.psum_scatter(
            grad_cross_key.astype(jnp.bfloat16), "head", scatter_dimension=0, tiled=True
        ).astype(jnp.float32),
        lax.psum_scatter(
            grad_cross_value.astype(jnp.bfloat16), "head", scatter_dimension=0, tiled=True
        ).astype(jnp.float32),
        lax.psum_scatter(
            grad_cross_output.astype(jnp.bfloat16), "head", scatter_dimension=0, tiled=True
        ).astype(jnp.float32),
        lax.psum_scatter(
            grad_feed_gain.astype(jnp.bfloat16), "head", scatter_dimension=0, tiled=True
        ).astype(jnp.float32),
        lax.psum_scatter(
            grad_feed_in.astype(jnp.bfloat16), "head", scatter_dimension=0, tiled=True
        ).astype(jnp.float32),
        lax.psum_scatter(
            grad_feed_out.astype(jnp.bfloat16), "head", scatter_dimension=0, tiled=True
        ).astype(jnp.float32),
        lax.psum_scatter(
            grad_row.astype(jnp.bfloat16), "head", scatter_dimension=0, tiled=True
        ).astype(jnp.float32),
    )
    summed = tuple(
        lax.psum(
            (
                shards[0],
                shards[1],
                shards[2],
                shards[3],
                shards[4],
                shards[5],
                shards[6],
                shards[7],
                shards[8],
                shards[9],
                shards[10],
                shards[11],
                shards[12],
                shards[13],
                shards[14],
            ),
            "dp",
        )
    )
    return (residual_three.astype(jnp.bfloat16), ranking_score, grad_input, grad_encoder) + summed


def solution(mesh):
    in_specs = (
        P(("dp", "head"), None),
        P("dp", "head", None),
        P("dp", None),
        P("dp", None),
        P(),
        P(),
        P(),
        P(),
        P(),
        P(),
        P(),
        P(),
        P(),
        P(),
        P(),
        P(),
        P(),
        P(),
        P(),
        P(),
        P(("dp", "head"), None),
        P(("dp", "head")),
    )
    out_specs = (
        P(("dp", "head"), None),
        P(("dp", "head")),
        P(("dp", "head"), None),
        P("dp", "head", None),
        P("head"),
        P("head", None),
        P("head", None),
        P("head", None),
        P("head", None),
        P("head", None),
        P("head"),
        P("head", None),
        P("head", None),
        P("head", None),
        P("head", None),
        P("head"),
        P("head", None),
        P("head", None),
        P("head"),
    )
    return jax.shard_map(body, mesh=mesh, in_specs=in_specs, out_specs=out_specs, check_vma=False)
```

profile of v0, /device:TPU:0, one launch (start us, length us, event | category | flops | bytes accessed | tf_op | source)
XLA Modules:
  0.0 899.2 jit_solution(10277776142889332813)
XLA Ops:
  13.5 4.3 all-to-all-start
  39.5 4.4 fusion.106
  45.1 4.4 all-to-all-start.2
  64.4 5.2 all-to-all-done.2
  87.6 16.6 %while.26 = (s32[]{:T(128)}, bf16[2,2,256,3,64]{2,4,3,1,0:T(8,128)(2,1)}, f32[2,2,3,256]{3,2,1,0:T(4,128)}, bf16[2,2,1024,3,64]{2,4,3,1,0:T(8,128)(2,1)}, s32[2,...) while((s32[]{:T(128)}, ...), condition=%wide.region_7.8_spmd, body=%wide.region_4.7_spmd.sunk | while | flops 423623168 | bytes 32762100 | solution.py:57
  104.2 4.5 all-to-all-start.3
  110.0 6.2 all-to-all-done.3
  136.5 4.1 all-to-all-start.4
  143.7 4.4 all-to-all-done.4
  148.9 31.2 %while.27 = (s32[]{:T(128)}, bf16[2,2,256,3,64]{2,4,3,1,0:T(8,128)(2,1)}, bf16[2,2,1024,3,64]{2,4,3,1,0:T(8,128)(2,1)}, bf16[2,2,1024,3,64]{2,4,3,1,0:T(8,128)(2...) while((s32[]{:T(128)}, ...), condition=%wide.region_13.14_spmd, body=%wide.region_11.13_spmd.sunk | while | flops 1023375872 | bytes 70765840 | solution.py:57
  180.1 10.9 %all_to_all.124 = bf16[4,256,192]{1,2,0:T(8,128)(2,1)S(1)} all-to-all(bf16[4,256,192]{1,2,0:T(8,128)(2,1)} %bitcast.256), channel_id=1, replica_groups=mesh['dp'=8,'head'=4] {'head'}, dimensions={0} | all-to-all | bytes 786432 | tf_op jit(solution)/shard_map/all_to_all | solution.py:260
  227.5 4.1 copy.159
  231.7 36.5 %all_to_all.125 = bf16[4,1024,192]{2,0,1:T(4,128)(2,1)} all-to-all(bf16[4,1024,192]{2,0,1:T(4,128)(2,1)} %copy.159), channel_id=1, replica_groups=mesh['dp'=8,'head'=4] {'head'}, dimensions={1} | all-to-all | bytes 3145728 | tf_op jit(solution)/shard_map/all_to_all | solution.py:268
  268.1 6.3 copy.161
  282.4 4.1 copy.162
  286.6 36.5 %all_to_all.126 = bf16[4,1024,192]{2,0,1:T(4,128)(2,1)} all-to-all(bf16[4,1024,192]{2,0,1:T(4,128)(2,1)} %copy.162), channel_id=1, replica_groups=mesh['dp'=8,'head'=4] {'head'}, dimensions={1} | all-to-all | bytes 3145728 | tf_op jit(solution)/shard_map/all_to_all | solution.py:275
  323.0 6.3 copy.164
  337.4 5.3 convolution_convert_fusion.1
  343.3 6.6 convolution_convert_fusion
  361.6 10.7 %all-reduce.6 = (bf16[768]{0:T(1024)(128)(2,1)S(1)}, bf16[32,12]{1,0:T(8,128)(2,1)S(1)}, bf16[768]{0:T(1024)(128)(2,1)S(1)}, bf16[768]{0:T(1024)(128)(2,1)S(1)}, bf16[768]{0:T(1024)(128)(2,1)S(1)}) all-reduce(bf16[768]{0:T(1024)(128)(2,1)S(1)} %get-tuple-element.225, ...), channel_id=2, replica_groups=mesh['dp'=8,'head'=4] {'head'}, use_global_device_ids=true, to_apply=%region_18.19.clone | all-reduce | flops 3456 | bytes 13824
  382.7 22.0 %reduce-scatter.33.cloned.1.call-done = bf16[192,768]{1,0:T(8,128)(2,1)} async-done(((bf16[768,768]{1,0:T(8,128)(2,1)}), bf16[192,768]{1,0:T(8,128)(2,1)}) %reduce-scatter.33.cloned.1.call-update) | async-done | bytes 294928
  405.8 49.3 %reduce-scatter.27.cloned.1.call-done = bf16[192,3072]{1,0:T(8,128)(2,1)} async-done(((bf16[768,3072]{1,0:T(8,128)(2,1)}), bf16[192,3072]{1,0:T(8,128)(2,1)}) %reduce-scatter.27.cloned.1.call-update) | async-done | bytes 1179664 | tf_op jit(solution)/shard_map/reduce_scatter | solution.py:380
  455.1 50.4 %reduce-scatter.29.cloned.1.call-done = bf16[768,768]{1,0:T(8,128)(2,1)} async-done(((bf16[3072,768]{1,0:T(8,128)(2,1)}), bf16[768,768]{1,0:T(8,128)(2,1)}) %reduce-scatter.29.cloned.1.call-update) | async-done | bytes 1179664 | tf_op jit(solution)/shard_map/reduce_scatter | solution.py:383
  505.5 383.1 %all-reduce.8 = (f32[192]{0:T(256)}, f32[192,768]{1,0:T(8,128)}, f32[192,768]{1,0:T(8,128)}, f32[192,768]{1,0:T(8,128)}, f32[192,768]{1,0:T(8,128)}, /*index=5*/...) all-reduce(f32[192]{0:T(256)S(1)} %copy-done.69, ...), channel_id=1, replica_groups=mesh['dp'=8,'head'=4] {'dp'}, use_global_device_ids=true, to_apply=%region_19.20 | all-reduce | flops 2360160 | bytes 14162688 | tf_op jit(solution)/shard_map/psum | solution.py:391
  (354 shorter events, 212.3 us)
Async XLA Ops:
  13.5 30.5 %all-to-all-start = ((bf16[4,256,768]{1,0,2:T(4,128)(2,1)}), bf16[4,256,768]{1,0,2:T(4,128)(2,1)S(1)}, u32[]{:S(2)}, u32[]{:S(2)}) async-start(bf16[4,256,768]{1,0,2:T(4,128)(2,1)} %copy.142), calls=%async_computation | async-start | bytes 3145728 | tf_op jit(solution)/shard_map/all_to_all | solution.py:209
  18.6 30.9 %copy-start.54 = (f32[256]{0:T(256)}, f32[256]{0:T(256)S(1)}, u32[]{:S(2)}) copy-start(f32[256]{0:T(256)S(1)} %fusion.91) | copy-start | bytes 3076
  45.1 24.5 %all-to-all-start.2 = ((bf16[4,256,768]{1,0,2:T(4,128)(2,1)}), bf16[4,256,768]{1,0,2:T(4,128)(2,1)}, u32[]{:S(2)}, u32[]{:S(2)}) async-start(bf16[4,256,768]{1,0,2:T(4,128)(2,1)} %copy.146), calls=%async_computation.2 | async-start | bytes 3145728 | tf_op jit(solution)/shard_map/all_to_all | solution.py:208
  61.2 12.1 %copy-start.72 = (s32[4,16]{1,0:T(4,128)S(1)}, s32[4,16]{1,0:T(4,128)}, u32[]{:S(2)}) copy-start(s32[4,16]{1,0:T(4,128)} %param.29) | copy-start | bytes 772
  61.2 15.0 %copy-start.13 = (bf16[4,256,768]{1,0,2:T(4,128)(2,1)S(1)}, bf16[4,256,768]{1,0,2:T(4,128)(2,1)}, u32[]{:S(2)}) copy-start(bf16[4,256,768]{1,0,2:T(4,128)(2,1)} %copy-done.12) | copy-start | bytes 4718596
  69.6 17.2 %all-to-all-start.1 = ((bf16[256,4,192]{0,2,1:T(8,128)(2,1)}), bf16[256,4,192]{0,2,1:T(8,128)(2,1)S(1)}, u32[]{:S(2)}, u32[]{:S(2)}) async-start(bf16[256,4,192]{0,2,1:T(8,128)(2,1)} %bitcast.254), calls=%async_computation.1 | async-start | bytes 786432 | tf_op jit(solution)/shard_map/all_to_all | solution.py:206
  104.2 12.0 %all-to-all-start.3 = ((bf16[4,256,192]{1,2,0:T(8,128)(2,1)}), bf16[4,256,192]{1,2,0:T(8,128)(2,1)}, u32[]{:S(2)}, u32[]{:S(2)}) async-start(bf16[4,256,192]{1,2,0:T(8,128)(2,1)} %bitcast.257), calls=%async_computation.3 | async-start | bytes 786432 | tf_op jit(solution)/shard_map/all_to_all | solution.py:222
  118.5 10.3 %copy-start.8 = (f32[256,768]{1,0:T(8,128)}, f32[256,768]{1,0:T(8,128)S(1)}, u32[]{:S(2)}) copy-start(f32[256,768]{1,0:T(8,128)S(1)} %get-tuple-element.302) | copy-start | bytes 2359300
  136.5 11.6 %all-to-all-start.4 = ((bf16[256,4,192]{0,2,1:T(8,128)(2,1)}), bf16[256,4,192]{0,2,1:T(8,128)(2,1)}, u32[]{:S(2)}, u32[]{:S(2)}) async-start(bf16[256,4,192]{0,2,1:T(8,128)(2,1)} %bitcast.255), calls=%async_computation.4 | async-start | bytes 786432 | tf_op jit(solution)/shard_map/all_to_all | solution.py:245
  140.6 240.9 %reduce-scatter.25.cloned.1.call-start = ((), (), s32[]{:S(2)}) async-start(), calls=%async_computation.23 | async-start | bytes 1474560 | tf_op jit(solution)/shard_map/reduce_scatter | solution.py:374
  143.5 238.0 %reduce-scatter.23.cloned.1.call-start = ((), (), s32[]{:S(2)}) async-start(), calls=%async_computation.22 | async-start | bytes 1474560 | tf_op jit(solution)/shard_map/reduce_scatter | solution.py:365
  194.7 186.8 %reduce-scatter.19.cloned.1.call-start = ((), (), s32[]{:S(2)}) async-start(), calls=%async_computation.20 | async-start | bytes 1474560 | tf_op jit(solution)/shard_map/reduce_scatter | solution.py:353
  207.9 173.6 %reduce-scatter.21.cloned.1.call-start = ((), (), s32[]{:S(2)}) async-start(), calls=%async_computation.21 | async-start | bytes 1474560 | tf_op jit(solution)/shard_map/reduce_scatter | solution.py:356
  209.6 172.0 %reduce-scatter.17.cloned.1.call-start = ((), (), s32[]{:S(2)}) async-start(), calls=%async_computation.19 | async-start | bytes 1474560 | tf_op jit(solution)/shard_map/reduce_scatter | solution.py:350
  220.9 160.6 %reduce-scatter.15.cloned.1.call-start = ((), (), s32[]{:S(2)}) async-start(), calls=%async_computation.18 | async-start | bytes 1474560 | tf_op jit(solution)/shard_map/reduce_scatter | solution.py:347
  227.5 154.1 %reduce-scatter.31.cloned.1.call-start = ((), (), s32[]{:S(2)}) async-start(), calls=%async_computation.26 | async-start | bytes 1474560
  282.4 122.3 %reduce-scatter.33.cloned.1.call-start = ((), (), s32[]{:S(2)}) async-start(), calls=%async_computation.27 | async-start | bytes 1474560
  337.3 117.8 %reduce-scatter.27.cloned.1.call-start = ((), (), s32[]{:S(2)}) async-start(), calls=%async_computation.24 | async-start | bytes 5898240 | tf_op jit(solution)/shard_map/reduce_scatter | solution.py:380
  342.7 162.9 %reduce-scatter.29.cloned.1.call-start = ((), (), s32[]{:S(2)}) async-start(), calls=%async_computation.25 | async-start | bytes 5898240 | tf_op jit(solution)/shard_map/reduce_scatter | solution.py:383
  360.2 14.1 %copy-start.65 = (f32[256]{0:T(256)S(1)}, f32[256]{0:T(256)}, u32[]{:S(2)}) copy-start(f32[256]{0:T(256)} %copy-done.64) | copy-start | bytes 3076
  378.3 127.2 %copy-start.67 = (f32[192]{0:T(256)S(1)}, f32[192]{0:T(256)}, u32[]{:S(2)}) copy-start(f32[192]{0:T(256)} %dynamic-slice_convert_fusion.2) | copy-start | bytes 2308
  378.3 127.2 %copy-start.68 = (f32[192]{0:T(256)S(1)}, f32[192]{0:T(256)}, u32[]{:S(2)}) copy-start(f32[192]{0:T(256)} %dynamic-slice_convert_fusion.3) | copy-start | bytes 2308
  378.3 127.2 %copy-start.69 = (f32[192]{0:T(256)S(1)}, f32[192]{0:T(256)}, u32[]{:S(2)}) copy-start(f32[192]{0:T(256)} %dynamic-slice_convert_fusion.4) | copy-start | bytes 2308
  381.5 124.1 %copy-start.42 = (bf16[192,768]{1,0:T(8,128)(2,1)S(1)}, bf16[192,768]{1,0:T(8,128)(2,1)}, u32[]{:S(2)}) copy-start(bf16[192,768]{1,0:T(8,128)(2,1)} %reduce-scatter.25.cloned.1.call-done) | copy-start | bytes 884740
  (88 other events, 248.6 us)
Sparse Core Ops, SparseCore 0:
  144.0 28.2 reduce-scatter.24
  194.8 26.8 reduce-scatter.22
  224.3 32.1 reduce-scatter.18
  259.0 25.7 reduce-scatter.20
  287.2 32.1 reduce-scatter.16
  322.0 25.7 reduce-scatter.14
  350.3 25.7 reduce-scatter.30
  378.9 25.7 reduce-scatter.32
  407.2 47.8 reduce-scatter.26
  457.6 47.8 reduce-scatter.28
where the time goes:
time: 910 us; the launch traced here: 899 us
  blocking collectives  478 us (53%)
  waiting for transfers between devices  138 us (15%)
  matrix products  124 us (14%)
  local copies, waits for them, and re-layouts  105 us (12%)
  starting transfers between devices  22.1 us (2%)
  between operations  16.9 us (2%)
  other arithmetic  16.3 us (2%)
    psum x1, blocking collectives, body(): lax.psum((shards[0], shards[1], shards[2], shards[3], shards[4], shards[5...  383 us
    reduce_scatter x1, waiting for transfers between devices, body(): lax.psum_scatter(grad_feed_out.astype(jnp.bfloat16), 'head', scatter_dime...  50.4 us
    reduce_scatter x1, waiting for transfers between devices, body(): lax.psum_scatter(grad_feed_in.astype(jnp.bfloat16), 'head', scatter_dimen...  49.3 us
    all_to_all x1, blocking collectives, body(): lax.all_to_all(grad_key.astype(jnp.bfloat16).reshape(row_count, key_len,...  36.5 us
    all_to_all x1, blocking collectives, body(): lax.all_to_all(grad_value.astype(jnp.bfloat16).reshape(row_count, key_len...  36.5 us
    dot_general x10, matrix products, contract_rows(): lax.dot_general(first_factor, second_factor, (((0,), (0,)), ((), ())), pr...  29.9 us
    unnamed x163, local copies, waits for them, and re-layouts  26.4 us
    dot_general x10, matrix products, matmul(): jnp.dot(first_factor, second_factor, preferred_element_type=jnp.float32)  25.9 us
  transfers between devices with their start and end apart: 15, of which 6 were waited for; matrix products, arithmetic and copies ran while one was open for 21% of the time, Pallas kernels for 0%

commit v1 on v0

--- a/solution.py
+++ b/solution.py
@@ -37,25 +37,6 @@
     return lax.dot_general(
         first_factor, second_factor, (((1,), (1,)), ((), ())), preferred_element_type=jnp.float32
     )
-
-
-def block_rows(row_count, per_row):
-    target = max(1, -(-512 // per_row))
-    chosen = row_count
-    for option in range(row_count, 0, -1):
-        if row_count % option == 0 and option >= target:
-            chosen = option
-    return chosen
-
-
-def by_blocks(function, arrays, rows_each):
-    row_total = arrays[0].shape[0]
-    block_count = row_total // rows_each
-    shaped = tuple(
-        (member.reshape((block_count, rows_each) + member.shape[1:]) for member in arrays)
-    )
-    results = lax.map(lambda members: function(*members), shaped)
-    return jax.tree.map(lambda member: member.reshape((row_total,) + member.shape[2:]), results)
 
 
 def masked_scores(query_heads, key_heads, query_segment, key_segment):
@@ -123,6 +104,96 @@
         grad_weights,
         jnp.sum(weights * grad_weights, axis=-1),
     )
+
+
+def ring_maps(dp_size, head_size):
+    length = dp_size // 2
+
+    def of(move):
+        pairs = []
+        for outer in range(dp_size):
+            for inner in range(head_size):
+                goal = move(outer, inner)
+                if goal is not None:
+                    pairs.append((outer * head_size + inner, goal[0] * head_size + goal[1]))
+        return pairs
+
+    def along(move):
+        def step(outer, inner):
+            spot = move(outer // 2)
+            return None if spot is None else (spot * 2 + outer % 2, inner)
+
+        return of(step)
+
+    half = length // 2
+    inward = [
+        along(
+            lambda spot, step=step: spot + 1
+            if spot == step
+            else (spot - 1 if spot == length - 1 - step else None)
+        )
+        for step in range(half - 1)
+    ]
+    middle = along(
+        lambda spot: length - 1 - spot if spot in (half - 1, half) else None
+    )
+    outward = [
+        along(
+            lambda spot, step=step: spot - 1
+            if spot == step + 1
+            else (spot + 1 if spot == length - 2 - step else None)
+        )
+        for step in range(half - 1)
+    ]
+    return {
+        "core": of(lambda outer, inner: (outer, inner ^ 1)),
+        "chip": of(lambda outer, inner: (outer, inner ^ 2)),
+        "cross": of(lambda outer, inner: (outer, inner ^ 3)),
+        "pair": of(lambda outer, inner: (outer ^ 1, inner)),
+        "inward": inward,
+        "middle": middle,
+        "outward": outward,
+    }
+
+
+AXES = ("dp", "head")
+
+
+def add_low(first, second):
+    return (first.astype(jnp.float32) + second.astype(jnp.float32)).astype(jnp.bfloat16)
+
+
+def line_sum(part, maps, line):
+    for perm in maps["inward"]:
+        part = add_low(part, lax.ppermute(part, AXES, perm))
+    part = add_low(part, lax.ppermute(part, AXES, maps["middle"]))
+    length = lax.axis_size("dp") // 2
+    for step in range(len(maps["outward"]) - 1, -1, -1):
+        came = lax.ppermute(part, AXES, maps["outward"][step])
+        takes = (line == step) | (line == length - 1 - step)
+        part = jnp.where(takes, came, part)
+    return part
+
+
+def reduce_weight(partial, maps, place):
+    chip, core, pair, line = place
+    rows = partial.shape[0] // 4
+    parts = partial.astype(jnp.bfloat16).reshape(2, 2, rows, partial.shape[1])
+    mine = lax.dynamic_index_in_dim(parts, core, 1, keepdims=False)
+    other = lax.dynamic_index_in_dim(parts, 1 - core, 1, keepdims=False)
+    both = add_low(mine, lax.ppermute(other, AXES, maps["core"]))
+    keep = lax.dynamic_index_in_dim(both, chip, 0, keepdims=False)
+    send = lax.dynamic_index_in_dim(both, 1 - chip, 0, keepdims=False)
+    group = add_low(keep, lax.ppermute(send, AXES, maps["chip"]))
+    halves = group.reshape(2, rows // 2, partial.shape[1])
+    keep = lax.dynamic_index_in_dim(halves, pair, 0, keepdims=False)
+    send = lax.dynamic_index_in_dim(halves, 1 - pair, 0, keepdims=False)
+    half = add_low(keep, lax.ppermute(send, AXES, maps["pair"]))
+    total = line_sum(half, maps, line)
+    came = lax.ppermute(total, AXES, maps["pair"])
+    first = jnp.where(pair == 0, total, came)
+    second = jnp.where(pair == 0, came, total)
+    return jnp.concatenate([first, second], axis=0).astype(jnp.float32)
 
 
 def body(
@@ -160,10 +231,26 @@
     group_size = lax.axis_size("head")
     row_count = encoder_out.shape[0]
     part_len = encoder_out.shape[1]
-    pair_count = slot_segment.shape[1]
-    per_row = pair_count * step_count
-    rows_each = block_rows(row_count, per_row)
     score_scale = head_width ** (-0.5)
+    maps = ring_maps(lax.axis_size("dp"), group_size)
+    head_index = lax.axis_index("head")
+    dp_index = lax.axis_index("dp")
+    place = (head_index // 2, head_index % 2, dp_index % 2, dp_index // 2)
+    blocks = [lax.dynamic_index_in_dim(encoder_out, head_index ^ near, 0, keepdims=False) for near in range(4)]
+    encoder_rows = jnp.concatenate(
+        [blocks[0]]
+        + [
+            lax.ppermute(blocks[near], AXES, maps[name])
+            for near, name in ((1, "core"), (2, "chip"), (3, "cross"))
+        ],
+        axis=0,
+    )
+    own_slots = lax.dynamic_index_in_dim(slot_segment, head_index, 0, keepdims=False)
+    own_segment = lax.dynamic_index_in_dim(encoder_segment, head_index, 0, keepdims=False)
+    own_segment = own_segment.reshape(group_size, part_len)
+    key_segment = jnp.stack(
+        [lax.dynamic_index_in_dim(own_segment, head_index ^ near, 0, keepdims=False) for near in range(4)]
+    ).reshape(1, -1)
 
     def slot_heads(matrix):
         return matrix.reshape(slot_count, step_count, head_count, head_width)
@@ -191,35 +278,17 @@
     residual_one = tokens + matmul(mixed_one, self_output)
     act_two = rms_norm(residual_one, cross_gain).astype(jnp.bfloat16)
     query_two = matmul(act_two, cross_query).astype(jnp.bfloat16)
-    encoder_rows = encoder_out.reshape(row_count * part_len, model_width)
-    key_two = (
-        matmul(encoder_rows, cross_key)
-        .astype(jnp.bfloat16)
-        .reshape(row_count, part_len, model_width)
-    )
-    value_two = (
-        matmul(encoder_rows, cross_value)
-        .astype(jnp.bfloat16)
-        .reshape(row_count, part_len, model_width)
-    )
-    query_segment = jnp.repeat(slot_segment, step_count, axis=1)
-    group_query = lax.all_to_all(query_two, "head", split_axis=1, concat_axis=0, tiled=True)
-    group_key, group_value = (
-        lax.all_to_all(key_two, "head", split_axis=2, concat_axis=1, tiled=True),
-        lax.all_to_all(value_two, "head", split_axis=2, concat_axis=1, tiled=True),
-    )
-    local_heads = head_count // group_size
-    key_len = group_key.shape[1]
-    query_heads = group_query.reshape(row_count, per_row, local_heads, head_width)
-    key_heads = group_key.reshape(row_count, key_len, local_heads, head_width)
-    value_heads = group_value.reshape(row_count, key_len, local_heads, head_width)
-    outputs, log_totals = by_blocks(
-        attend_whole,
-        (query_heads, key_heads, value_heads, query_segment, encoder_segment),
-        rows_each,
-    )
-    outputs = outputs.astype(jnp.bfloat16).reshape(group_size * tok_count, local_heads * head_width)
-    mixed_two = lax.all_to_all(outputs, "head", split_axis=0, concat_axis=1, tiled=True)
+    key_len = group_size * part_len
+    key_two = matmul(encoder_rows, cross_key).astype(jnp.bfloat16)
+    value_two = matmul(encoder_rows, cross_value).astype(jnp.bfloat16)
+    query_segment = jnp.repeat(own_slots, step_count)[None, :]
+    local_query = query_two.reshape(1, tok_count, head_count, head_width)
+    key_heads = key_two.reshape(1, key_len, head_count, head_width)
+    value_heads = value_two.reshape(1, key_len, head_count, head_width)
+    outputs, log_totals = attend_whole(
+        local_query, key_heads, value_heads, query_segment, key_segment
+    )
+    mixed_two = outputs.astype(jnp.bfloat16).reshape(tok_count, model_width)
     residual_two = residual_one + matmul(mixed_two, cross_output)
     act_three = rms_norm(residual_two, feed_gain).astype(jnp.bfloat16)
     pre_act = matmul(act_three, feed_in)
@@ -242,52 +311,27 @@
     grad_two_low = grad_two.astype(jnp.bfloat16)
     grad_cross_output = contract_rows(mixed_two, grad_two_low)
     grad_mixed = contract_cols(grad_two_low, cross_output).astype(jnp.bfloat16)
-    group_grad = lax.all_to_all(grad_mixed, "head", split_axis=1, concat_axis=0, tiled=True)
-    grad_heads = group_grad.reshape(row_count, per_row, local_heads, head_width)
-    grad_query, grad_key, grad_value = by_blocks(
-        local_grads,
-        (
-            query_heads,
-            key_heads,
-            value_heads,
-            grad_heads,
-            query_segment,
-            encoder_segment,
-            log_totals,
-        ),
-        rows_each,
-    )
-    query_back = lax.all_to_all(
-        grad_query.astype(jnp.bfloat16).reshape(group_size * tok_count, local_heads * head_width),
-        "head",
-        split_axis=0,
-        concat_axis=1,
-        tiled=True,
-    )
-    key_back, value_back = (
-        lax.all_to_all(
-            grad_key.astype(jnp.bfloat16).reshape(row_count, key_len, local_heads * head_width),
-            "head",
-            split_axis=1,
-            concat_axis=2,
-            tiled=True,
-        ),
-        lax.all_to_all(
-            grad_value.astype(jnp.bfloat16).reshape(row_count, key_len, local_heads * head_width),
-            "head",
-            split_axis=1,
-            concat_axis=2,
-            tiled=True,
-        ),
-    )
+    grad_heads = grad_mixed.reshape(1, tok_count, head_count, head_width)
+    grad_query, grad_key, grad_value = local_grads(
+        local_query, key_heads, value_heads, grad_heads, query_segment, key_segment, log_totals
+    )
+    query_back = grad_query.astype(jnp.bfloat16).reshape(tok_count, model_width)
+    key_flat = grad_key.astype(jnp.bfloat16).reshape(key_len, model_width)
+    value_flat = grad_value.astype(jnp.bfloat16).reshape(key_len, model_width)
     grad_cross_query = contract_rows(act_two, query_back)
-    key_flat = key_back.reshape(row_count * part_len, model_width)
-    value_flat = value_back.reshape(row_count * part_len, model_width)
     grad_cross_key = contract_rows(encoder_rows, key_flat)
     grad_cross_value = contract_rows(encoder_rows, value_flat)
-    grad_encoder = (
-        contract_cols(key_flat, cross_key) + contract_cols(value_flat, cross_value)
-    ).reshape(row_count, part_len, model_width)
+    grad_rows = contract_cols(key_flat, cross_key) + contract_cols(value_flat, cross_value)
+    grad_rows = grad_rows.reshape(group_size, part_len, model_width)
+    pieces = [grad_rows[0]] + [
+        lax.ppermute(grad_rows[near].astype(jnp.bfloat16), AXES, maps[name]).astype(jnp.float32)
+        for near, name in ((1, "core"), (2, "chip"), (3, "cross"))
+    ]
+    grad_encoder = jnp.zeros((row_count, part_len, model_width), jnp.float32)
+    for near in range(group_size):
+        grad_encoder = lax.dynamic_update_index_in_dim(
+            grad_encoder, pieces[near], head_index ^ near, 0
+        )
     grad_norm_two, grad_cross_gain = norm_back(
         residual_one, cross_gain, contract_cols(query_back, cross_query)
     )
@@ -340,76 +384,31 @@
     )
     grad_norm_one, grad_self_gain = norm_back(tokens, self_gain, upstream_one)
     grad_input = grad_one + grad_norm_one
-    shards = (
-        lax.psum_scatter(
-            grad_self_gain.astype(jnp.bfloat16), "head", scatter_dimension=0, tiled=True
-        ).astype(jnp.float32),
-        lax.psum_scatter(
-            grad_self_query.astype(jnp.bfloat16), "head", scatter_dimension=0, tiled=True
-        ).astype(jnp.float32),
-        lax.psum_scatter(
-            grad_self_key.astype(jnp.bfloat16), "head", scatter_dimension=0, tiled=True
-        ).astype(jnp.float32),
-        lax.psum_scatter(
-            grad_self_value.astype(jnp.bfloat16), "head", scatter_dimension=0, tiled=True
-        ).astype(jnp.float32),
-        lax.psum_scatter(
-            grad_self_output.astype(jnp.bfloat16), "head", scatter_dimension=0, tiled=True
-        ).astype(jnp.float32),
-        lax.psum_scatter(
-            grad_bias.astype(jnp.bfloat16), "head", scatter_dimension=0, tiled=True
-        ).astype(jnp.float32),
-        lax.psum_scatter(
-            grad_cross_gain.astype(jnp.bfloat16), "head", scatter_dimension=0, tiled=True
-        ).astype(jnp.float32),
-        lax.psum_scatter(
-            grad_cross_query.astype(jnp.bfloat16), "head", scatter_dimension=0, tiled=True
-        ).astype(jnp.float32),
-        lax.psum_scatter(
-            grad_cross_key.astype(jnp.bfloat16), "head", scatter_dimension=0, tiled=True
-        ).astype(jnp.float32),
-        lax.psum_scatter(
-            grad_cross_value.astype(jnp.bfloat16), "head", scatter_dimension=0, tiled=True
-        ).astype(jnp.float32),
-        lax.psum_scatter(
-            grad_cross_output.astype(jnp.bfloat16), "head", scatter_dimension=0, tiled=True
-        ).astype(jnp.float32),
-        lax.psum_scatter(
-            grad_feed_gain.astype(jnp.bfloat16), "head", scatter_dimension=0, tiled=True
-        ).astype(jnp.float32),
-        lax.psum_scatter(
-            grad_feed_in.astype(jnp.bfloat16), "head", scatter_dimension=0, tiled=True
-        ).astype(jnp.float32),
-        lax.psum_scatter(
-            grad_feed_out.astype(jnp.bfloat16), "head", scatter_dimension=0, tiled=True
-        ).astype(jnp.float32),
-        lax.psum_scatter(
-            grad_row.astype(jnp.bfloat16), "head", scatter_dimension=0, tiled=True
-        ).astype(jnp.float32),
-    )
-    summed = tuple(
-        lax.psum(
-            (
-                shards[0],
-                shards[1],
-                shards[2],
-                shards[3],
-                shards[4],
-                shards[5],
-                shards[6],
-                shards[7],
-                shards[8],
-                shards[9],
-                shards[10],
-                shards[11],
-                shards[12],
-                shards[13],
-                shards[14],
-            ),
-            "dp",
-        )
-    )
-    return (residual_three.astype(jnp.bfloat16), ranking_score, grad_input, grad_encoder) + summed
+    small = jnp.concatenate(
+        [member.reshape(group_size, -1) for member in (grad_self_gain, grad_bias, grad_cross_gain, grad_feed_gain, grad_row)], axis=1
+    )
+    small = lax.psum(lax.psum_scatter(small, "head", scatter_dimension=0, tiled=True), "dp")[0]
+    width = model_width // group_size
+    bias_size = grad_bias.size // group_size
+    sums = [reduce_weight(member, maps, place) for member in (
+        grad_self_query, grad_self_key, grad_self_value, grad_self_output,
+        grad_cross_query, grad_cross_key, grad_cross_value, grad_cross_output,
+        grad_feed_in, grad_feed_out)]
+    rest = width + bias_size
+    return (
+        residual_three.astype(jnp.bfloat16),
+        ranking_score,
+        grad_input,
+        grad_encoder,
+        small[:width],
+        *sums[:4],
+        small[width:rest].reshape(-1, head_count),
+        small[rest : rest + width],
+        *sums[4:8],
+        small[rest + width : rest + 2 * width],
+        *sums[8:],
+        small[rest + 2 * width :],
+    )
 
 
 def solution(mesh):

time: 910 us -> 524 us (0.58); the launches traced: 899 us -> 524 us
  blocking collectives: 478 us -> 45.8 us
  waiting for transfers between devices: 138 us -> 195 us
  local copies, waits for them, and re-layouts: 105 us -> 51.3 us
  starting transfers between devices: 22.1 us -> 68.9 us
  other arithmetic: 16.3 us -> 42.4 us
  between operations: 16.9 us -> 3.25 us
    psum x1, blocking collectives: 383 us -> 21.7 us  [body(): lax.psum(lax.psum_scatter(small, 'head', scatter_dimension=0, tiled=True)...]
    ppermute x0 -> x76, waiting for transfers between devices: none -> 195 us  [the longest x10 86.3 us: reduce_weight(): group = add_low(keep, lax.ppermute(send, AXES, maps['chip']))]
    reduce_scatter x8 -> x0, waiting for transfers between devices: 99.8 us -> none  [the longest x1 50.4 us: body(): lax.psum_scatter(grad_feed_out.astype(jnp.bfloat16), 'head', scatter_dime...]
    all_to_all x3 -> x0, blocking collectives: 83.8 us -> none  [the longest x1 36.5 us: body(): lax.all_to_all(grad_key.astype(jnp.bfloat16).reshape(row_count, key_len,...]
    ppermute x0 -> x76, starting transfers between devices: none -> 68.9 us  [the longest x10 22.6 us: line_sum(): part = add_low(part, lax.ppermute(part, AXES, perm))]
    unnamed x12 -> x0, waiting for transfers between devices: 22.1 us -> none
    all_to_all x5 -> x0, starting transfers between devices: 21 us -> none  [the longest x1 4.52 us: body(): lax.all_to_all(outputs, 'head', split_axis=0, concat_axis=1, tiled=True)]
    all_to_all x6 -> x0, local copies, waits for them, and re-layouts: 18.1 us -> none  [the longest x1 6.34 us: body(): lax.all_to_all(grad_key.astype(jnp.bfloat16).reshape(row_count, key_len,...]
  transfers between devices with their start and end apart: 15 -> 76, of which waited for: 6 -> 36; matrix products, arithmetic and copies ran while one was open for 21% -> 14% of each run, Pallas kernels for 0% -> 0%
where the time goes in v1:
time: 524 us
  waiting for transfers between devices  195 us (37%)
  matrix products  118 us (23%)
  starting transfers between devices  68.9 us (13%)
  local copies, waits for them, and re-layouts  51.3 us (10%)
  blocking collectives  45.8 us (9%)
  other arithmetic  42.4 us (8%)
    ppermute x10, waiting for transfers between devices, reduce_weight(): group = add_low(keep, lax.ppermute(send, AXES, maps['chip']))  86.3 us
    ppermute x10, waiting for transfers between devices, line_sum(): came = lax.ppermute(part, AXES, maps['outward'][step])  57.5 us
    dot_general x10, matrix products, contract_cols(): lax.dot_general(first_factor, second_factor, (((1,), (1,)), ((), ())), pr...  34.3 us
    dot_general x10, matrix products, contract_rows(): lax.dot_general(first_factor, second_factor, (((0,), (0,)), ((), ())), pr...  25.1 us
    unnamed x1, blocking collectives  24.1 us
    ppermute x10, starting transfers between devices, line_sum(): part = add_low(part, lax.ppermute(part, AXES, perm))  22.6 us
    ppermute x10, waiting for transfers between devices, reduce_weight(): half = add_low(keep, lax.ppermute(send, AXES, maps['pair']))  22.4 us
    psum x1, blocking collectives, body(): lax.psum(lax.psum_scatter(small, 'head', scatter_dimension=0, tiled=True)...  21.7 us
  transfers between devices with their start and end apart: 76, of which 36 were waited for; matrix products, arithmetic and copies ran while one was open for 14% of the time, Pallas kernels for 0%

profile of v1, /device:TPU:0, one launch (start us, length us, event | category | flops | bytes accessed | tf_op | source)
XLA Modules:
  0.0 524.0 jit_solution(14371903701796995943)
XLA Ops:
  40.5 4.5 select_reduce_fusion
  54.7 16.5 %fusion.11 = bf16[256,3072]{1,0:T(8,128)(2,1)S(1)} fusion(f32[256,3072]{1,0:T(8,128)S(1)} %fusion.88, bf16[3072,768]{1,0:T(8,128)(2,1)S(1)} %bitcast.367, f32[256,768]{1,0:T(8,128)S(1)} %copy-done.97, f32[256]{0:T(256)S(1)} %get-tuple-element.85, f32[768]{0:T(1024)S(1)} %copy-done.88), kind=kOutput, calls=%fused_computation.22 | convolution fusion | flops 1224278016 | bytes 10227712 | tf_op jit(solution)/shard_map/dot_general | solution.py:37
  81.0 12.3 %multiply_reduce_fusion = (f32[12,256]{1,0:T(8,128)S(1)}, f32[12,256,1024]{2,1,0:T(8,128)}) fusion(f32[12,256]{1,0:T(8,128)} %copy-done.71, f32[12,256,1024]{2,1,0:T(8,128)} %copy-done.1, pred[256,1024]{1,0:T(8,128)(4,1)} %copy-done.27, bf16[256,12,64]{0,2,1:T(8,128)(2,1)} %bitcast.359, bf16[1024,12,64]{0,2,1:T(8,128)(2,1)} %bitcast.369), kind=kOutput, calls=%fused_computation.2 | convolution fusion | flops 421524480 | bytes 27418624 | tf_op jit(solution)/shard_map/rqhd,rkhd->rhqk/dot_general | solution.py:67
  94.2 7.1 %multiply_convert_fusion = bf16[12,256,1024]{2,1,0:T(8,128)(2,1)S(1)} fusion(f32[12,256,1024]{2,1,0:T(8,128)} %get-tuple-element.77, f32[12,256]{1,0:T(8,128)S(1)} %get-tuple-element.76, f32[12,256]{1,0:T(8,128)S(1)} %copy-done.72, f32[12,256,1024]{2,1,0:T(8,128)S(1)} %bitcast.292, pred[256,1024]{1,0:T(8,128)(4,1)S(1)} %copy-done.28), kind=kLoop, calls=%fused_computation.1 | loop fusion | flops 22020096 | bytes 31744000 | tf_op jit(solution)/shard_map/convert_element_type | solution.py:74
  120.6 4.7 convolution_convert_fusion.2
  143.5 4.5 convolution_convert_fusion
  167.5 24.1 %all-reduce = f32[4,864]{1,0:T(4,128)S(1)} all-reduce(f32[4,864]{1,0:T(4,128)S(1)} %concatenate.37), channel_id=2, replica_groups=mesh['dp'=8,'head'=4] {'head'}, use_global_device_ids=true, to_apply=%region_18.19.clone | all-reduce | flops 3456 | bytes 27648
  192.2 21.7 %psum.7 = f32[1,864]{1,0:T(1,128)S(1)} all-reduce(f32[1,864]{1,0:T(1,128)S(1)} %constant_dynamic-slice_fusion.6), channel_id=1, replica_groups=mesh['dp'=8,'head'=4] {'dp'}, use_global_device_ids=true, to_apply=%region_19.20 | all-reduce | flops 864 | bytes 6912 | tf_op jit(solution)/shard_map/psum | solution.py:390
  254.3 6.6 %collective-permute-done.7 = bf16[192,768]{1,0:T(8,128)(2,1)S(1)} collective-permute-done((bf16[192,768]{1,0:T(8,128)(2,1)S(1)}, bf16[192,768]{1,0:T(8,128)(2,1)S(1)}, u32[]{:S(2)}, u32[]{:S(2)}) %collective-permute-start.7) | collective-permute-done | bytes 294944 | tf_op jit(solution)/shard_map/ppermute | solution.py:187
  261.5 5.7 %collective-permute-done.14 = bf16[192,768]{1,0:T(8,128)(2,1)S(1)} collective-permute-done((bf16[192,768]{1,0:T(8,128)(2,1)S(1)}, bf16[192,768]{1,0:T(8,128)(2,1)S(1)}, u32[]{:S(2)}, u32[]{:S(2)}) %collective-permute-start.14) | collective-permute-done | bytes 294944 | tf_op jit(solution)/shard_map/ppermute | solution.py:187
  267.8 5.7 %collective-permute-done.21 = bf16[192,768]{1,0:T(8,128)(2,1)S(1)} collective-permute-done((bf16[192,768]{1,0:T(8,128)(2,1)S(1)}, bf16[192,768]{1,0:T(8,128)(2,1)S(1)}, u32[]{:S(2)}, u32[]{:S(2)}) %collective-permute-start.21) | collective-permute-done | bytes 294944 | tf_op jit(solution)/shard_map/ppermute | solution.py:187
  274.1 5.7 %collective-permute-done.28 = bf16[192,768]{1,0:T(8,128)(2,1)S(1)} collective-permute-done((bf16[192,768]{1,0:T(8,128)(2,1)S(1)}, bf16[192,768]{1,0:T(8,128)(2,1)S(1)}, u32[]{:S(2)}, u32[]{:S(2)}) %collective-permute-start.28) | collective-permute-done | bytes 294944 | tf_op jit(solution)/shard_map/ppermute | solution.py:187
  280.4 5.7 %collective-permute-done.35 = bf16[192,768]{1,0:T(8,128)(2,1)S(1)} collective-permute-done((bf16[192,768]{1,0:T(8,128)(2,1)S(1)}, bf16[192,768]{1,0:T(8,128)(2,1)S(1)}, u32[]{:S(2)}, u32[]{:S(2)}) %collective-permute-start.35) | collective-permute-done | bytes 294944 | tf_op jit(solution)/shard_map/ppermute | solution.py:187
  286.7 5.7 %collective-permute-done.42 = bf16[192,768]{1,0:T(8,128)(2,1)S(1)} collective-permute-done((bf16[192,768]{1,0:T(8,128)(2,1)S(1)}, bf16[192,768]{1,0:T(8,128)(2,1)S(1)}, u32[]{:S(2)}, u32[]{:S(2)}) %collective-permute-start.42) | collective-permute-done | bytes 294944 | tf_op jit(solution)/shard_map/ppermute | solution.py:187
  292.6 6.2 %collective-permute-done.49 = bf16[192,768]{1,0:T(8,128)(2,1)S(1)} collective-permute-done((bf16[192,768]{1,0:T(8,128)(2,1)S(1)}, bf16[192,768]{1,0:T(8,128)(2,1)S(1)}, u32[]{:S(2)}, u32[]{:S(2)}) %collective-permute-start.49) | collective-permute-done | bytes 294944 | tf_op jit(solution)/shard_map/ppermute | solution.py:187
  298.8 5.6 %collective-permute-done.56 = bf16[192,768]{1,0:T(8,128)(2,1)S(1)} collective-permute-done((bf16[192,768]{1,0:T(8,128)(2,1)S(1)}, bf16[192,768]{1,0:T(8,128)(2,1)S(1)}, u32[]{:S(2)}, u32[]{:S(2)}) %collective-permute-start.56) | collective-permute-done | bytes 294944 | tf_op jit(solution)/shard_map/ppermute | solution.py:187
  354.7 19.4 %collective-permute-done.11 = bf16[96,768]{1,0:T(8,128)(2,1)S(1)} collective-permute-done((bf16[96,768]{1,0:T(8,128)(2,1)S(1)}, bf16[96,768]{1,0:T(8,128)(2,1)S(1)}, u32[]{:S(2)}, u32[]{:S(2)}) %collective-permute-start.11) | collective-permute-done | bytes 147488 | tf_op jit(solution)/shard_map/ppermute | solution.py:172
  407.6 24.3 %collective-permute-done.63 = bf16[192,3072]{1,0:T(8,128)(2,1)S(1)} collective-permute-done((bf16[192,3072]{1,0:T(8,128)(2,1)S(1)}, bf16[192,3072]{1,0:T(8,128)(2,1)S(1)}, u32[]{:S(2)}, u32[]{:S(2)}) %collective-permute-start.63) | collective-permute-done | bytes 1179680 | tf_op jit(solution)/shard_map/ppermute | solution.py:187
  434.2 15.1 %collective-permute-done.70 = bf16[768,768]{1,0:T(8,128)(2,1)S(1)} collective-permute-done((bf16[768,768]{1,0:T(8,128)(2,1)S(1)}, bf16[768,768]{1,0:T(8,128)(2,1)S(1)}, u32[]{:S(2)}, u32[]{:S(2)}) %collective-permute-start.70) | collective-permute-done | bytes 1179680 | tf_op jit(solution)/shard_map/ppermute | solution.py:187
  454.2 6.6 %collective-permute-done.71 = bf16[384,768]{1,0:T(8,128)(2,1)S(1)} collective-permute-done((bf16[384,768]{1,0:T(8,128)(2,1)S(1)}, bf16[384,768]{1,0:T(8,128)(2,1)S(1)}, u32[]{:S(2)}, u32[]{:S(2)}) %collective-permute-start.71) | collective-permute-done | bytes 589856 | tf_op jit(solution)/shard_map/ppermute | solution.py:191
  468.5 4.6 collective-permute-done.72
  477.7 22.6 %collective-permute-done.67 = bf16[96,3072]{1,0:T(8,128)(2,1)S(1)} collective-permute-done((bf16[96,3072]{1,0:T(8,128)(2,1)S(1)}, bf16[96,3072]{1,0:T(8,128)(2,1)S(1)}, u32[]{:S(2)}, u32[]{:S(2)}) %collective-permute-start.67) | collective-permute-done | bytes 589856 | tf_op jit(solution)/shard_map/ppermute | solution.py:172
  509.3 6.5 %collective-permute-done.68 = bf16[96,3072]{1,0:T(8,128)(2,1)S(1)} collective-permute-done((bf16[96,3072]{1,0:T(8,128)(2,1)S(1)}, bf16[96,3072]{1,0:T(8,128)(2,1)S(1)}, u32[]{:S(2)}, u32[]{:S(2)}) %collective-permute-start.68) | collective-permute-done | bytes 589856 | tf_op jit(solution)/shard_map/ppermute | solution.py:193
  517.5 4.6 collective-permute-done.75
  (592 shorter events, 274.8 us)
Async XLA Ops:
  3.4 31.6 %collective-permute-start.2 = (bf16[256,768]{1,0:T(8,128)(2,1)}, bf16[256,768]{1,0:T(8,128)(2,1)}, u32[]{:S(2)}, u32[]{:S(2)}) collective-permute-start(bf16[256,768]{1,0:T(8,128)(2,1)} %get-tuple-element.34), channel_id=1, source_target_pairs={{0,3},{1,2},{2,1},{3,0},{4,7},{5,6},{6,5},{7,4},{8,11},{9,10},{10,... | collective-permute-start | bytes 1179656 | tf_op jit(solution)/shard_map/ppermute | solution.py:243
  5.8 29.2 %collective-permute-start.1 = (bf16[256,768]{1,0:T(8,128)(2,1)}, bf16[256,768]{1,0:T(8,128)(2,1)}, u32[]{:S(2)}, u32[]{:S(2)}) collective-permute-start(bf16[256,768]{1,0:T(8,128)(2,1)} %get-tuple-element.35), channel_id=1, source_target_pairs={{0,2},{1,3},{2,0},{3,1},{4,6},{5,7},{6,4},{7,5},{8,10},{9,11},{10,... | collective-permute-start | bytes 1179656 | tf_op jit(solution)/shard_map/ppermute | solution.py:243
  6.4 28.5 %collective-permute-start = (bf16[256,768]{1,0:T(8,128)(2,1)}, bf16[256,768]{1,0:T(8,128)(2,1)}, u32[]{:S(2)}, u32[]{:S(2)}) collective-permute-start(bf16[256,768]{1,0:T(8,128)(2,1)} %get-tuple-element.33), channel_id=1, source_target_pairs={{0,1},{1,0},{2,3},{3,2},{4,5},{5,4},{6,7},{7,6},{8,9},{9,8},{10,11... | collective-permute-start | bytes 1179656 | tf_op jit(solution)/shard_map/ppermute | solution.py:243
  164.5 73.9 %collective-permute-start.3 = (bf16[256,768]{1,0:T(8,128)(2,1)}, bf16[256,768]{1,0:T(8,128)(2,1)}, u32[]{:S(2)}, u32[]{:S(2)}) collective-permute-start(bf16[256,768]{1,0:T(8,128)(2,1)} %get-tuple-element.31), channel_id=1, source_target_pairs={{0,1},{1,0},{2,3},{3,2},{4,5},{5,4},{6,7},{7,6},{8,9},{9,8},{10,11... | collective-permute-start | bytes 1179656 | tf_op jit(solution)/shard_map/ppermute | solution.py:327
  164.9 75.7 %collective-permute-start.4 = (bf16[256,768]{1,0:T(8,128)(2,1)}, bf16[256,768]{1,0:T(8,128)(2,1)}, u32[]{:S(2)}, u32[]{:S(2)}) collective-permute-start(bf16[256,768]{1,0:T(8,128)(2,1)} %get-tuple-element.30), channel_id=1, source_target_pairs={{0,2},{1,3},{2,0},{3,1},{4,6},{5,7},{6,4},{7,5},{8,10},{9,11},{10,... | collective-permute-start | bytes 1179656 | tf_op jit(solution)/shard_map/ppermute | solution.py:327
  166.3 76.9 %collective-permute-start.5 = (bf16[256,768]{1,0:T(8,128)(2,1)}, bf16[256,768]{1,0:T(8,128)(2,1)}, u32[]{:S(2)}, u32[]{:S(2)}) collective-permute-start(bf16[256,768]{1,0:T(8,128)(2,1)} %get-tuple-element.29), channel_id=1, source_target_pairs={{0,3},{1,2},{2,1},{3,0},{4,7},{5,6},{6,5},{7,4},{8,11},{9,10},{10,... | collective-permute-start | bytes 1179656 | tf_op jit(solution)/shard_map/ppermute | solution.py:327
  216.6 28.6 %collective-permute-start.6 = (bf16[2,192,768]{2,1,0:T(8,128)(2,1)}, bf16[2,192,768]{2,1,0:T(8,128)(2,1)}, u32[]{:S(2)}, u32[]{:S(2)}) collective-permute-start(bf16[2,192,768]{2,1,0:T(8,128)(2,1)} %dynamic-slice_bitcast_fusion.13), channel_id=1, source_target_pairs={{0,1},{1,0},{2,3},{3,2},{4,5},{5,4},{6,7},{7,6},{8,9},{9,8},{10,11... | collective-permute-start | bytes 1769480 | tf_op jit(solution)/shard_map/ppermute | solution.py:184
  218.6 28.4 %collective-permute-start.13 = (bf16[2,192,768]{2,1,0:T(8,128)(2,1)}, bf16[2,192,768]{2,1,0:T(8,128)(2,1)}, u32[]{:S(2)}, u32[]{:S(2)}) collective-permute-start(bf16[2,192,768]{2,1,0:T(8,128)(2,1)} %dynamic-slice_bitcast_fusion.12), channel_id=1, source_target_pairs={{0,1},{1,0},{2,3},{3,2},{4,5},{5,4},{6,7},{7,6},{8,9},{9,8},{10,11... | collective-permute-start | bytes 1769480 | tf_op jit(solution)/shard_map/ppermute | solution.py:184
  249.3 150.6 %collective-permute-start.62 = (bf16[2,192,3072]{2,1,0:T(8,128)(2,1)S(1)}, bf16[2,192,3072]{2,1,0:T(8,128)(2,1)S(1)}, u32[]{:S(2)}, u32[]{:S(2)}) collective-permute-start(bf16[2,192,3072]{2,1,0:T(8,128)(2,1)S(1)} %copy-done.44), channel_id=1, source_target_pairs={{0,1},{1,0},{2,3},{3,2},{4,5},{5,4},{6,7},{7,6},{8,9},{9,8},{10,11... | collective-permute-start | bytes 7077896 | tf_op jit(solution)/shard_map/ppermute | solution.py:184
  250.4 155.7 %collective-permute-start.69 = (bf16[2,768,768]{2,1,0:T(8,128)(2,1)S(1)}, bf16[2,768,768]{2,1,0:T(8,128)(2,1)S(1)}, u32[]{:S(2)}, u32[]{:S(2)}) collective-permute-start(bf16[2,768,768]{2,1,0:T(8,128)(2,1)S(1)} %copy-done.43), channel_id=1, source_target_pairs={{0,1},{1,0},{2,3},{3,2},{4,5},{5,4},{6,7},{7,6},{8,9},{9,8},{10,11... | collective-permute-start | bytes 7077896 | tf_op jit(solution)/shard_map/ppermute | solution.py:184
  253.4 20.1 %collective-permute-start.21 = (bf16[192,768]{1,0:T(8,128)(2,1)S(1)}, bf16[192,768]{1,0:T(8,128)(2,1)S(1)}, u32[]{:S(2)}, u32[]{:S(2)}) collective-permute-start(bf16[192,768]{1,0:T(8,128)(2,1)S(1)} %dynamic-slice_bitcast_fusion.23), channel_id=1, source_target_pairs={{0,2},{1,3},{2,0},{3,1},{4,6},{5,7},{6,4},{7,5},{8,10},{9,11},{10,... | collective-permute-start | bytes 884744 | tf_op jit(solution)/shard_map/ppermute | solution.py:187
  260.8 19.0 %collective-permute-start.28 = (bf16[192,768]{1,0:T(8,128)(2,1)S(1)}, bf16[192,768]{1,0:T(8,128)(2,1)S(1)}, u32[]{:S(2)}, u32[]{:S(2)}) collective-permute-start(bf16[192,768]{1,0:T(8,128)(2,1)S(1)} %dynamic-slice_bitcast_fusion.22), channel_id=1, source_target_pairs={{0,2},{1,3},{2,0},{3,1},{4,6},{5,7},{6,4},{7,5},{8,10},{9,11},{10,... | collective-permute-start | bytes 884744 | tf_op jit(solution)/shard_map/ppermute | solution.py:187
  267.2 19.0 %collective-permute-start.35 = (bf16[192,768]{1,0:T(8,128)(2,1)S(1)}, bf16[192,768]{1,0:T(8,128)(2,1)S(1)}, u32[]{:S(2)}, u32[]{:S(2)}) collective-permute-start(bf16[192,768]{1,0:T(8,128)(2,1)S(1)} %dynamic-slice_bitcast_fusion.21), channel_id=1, source_target_pairs={{0,2},{1,3},{2,0},{3,1},{4,6},{5,7},{6,4},{7,5},{8,10},{9,11},{10,... | collective-permute-start | bytes 884744 | tf_op jit(solution)/shard_map/ppermute | solution.py:187
  350.7 23.4 %collective-permute-start.11 = (bf16[96,768]{1,0:T(8,128)(2,1)S(1)}, bf16[96,768]{1,0:T(8,128)(2,1)S(1)}, u32[]{:S(2)}, u32[]{:S(2)}) collective-permute-start(bf16[96,768]{1,0:T(8,128)(2,1)S(1)} %add_convert_fusion.18), channel_id=1, source_target_pairs={{8,0},{9,1},{10,2},{11,3},{12,4},{13,5},{14,6},{15,7},{16,24},{17,... | collective-permute-start | bytes 442376 | tf_op jit(solution)/shard_map/ppermute | solution.py:172
  352.0 25.2 %collective-permute-start.18 = (bf16[96,768]{1,0:T(8,128)(2,1)S(1)}, bf16[96,768]{1,0:T(8,128)(2,1)S(1)}, u32[]{:S(2)}, u32[]{:S(2)}) collective-permute-start(bf16[96,768]{1,0:T(8,128)(2,1)S(1)} %add_convert_fusion.16), channel_id=1, source_target_pairs={{8,0},{9,1},{10,2},{11,3},{12,4},{13,5},{14,6},{15,7},{16,24},{17,... | collective-permute-start | bytes 442376 | tf_op jit(solution)/shard_map/ppermute | solution.py:172
  353.4 27.0 %collective-permute-start.25 = (bf16[96,768]{1,0:T(8,128)(2,1)S(1)}, bf16[96,768]{1,0:T(8,128)(2,1)S(1)}, u32[]{:S(2)}, u32[]{:S(2)}) collective-permute-start(bf16[96,768]{1,0:T(8,128)(2,1)S(1)} %add_convert_fusion.14), channel_id=1, source_target_pairs={{8,0},{9,1},{10,2},{11,3},{12,4},{13,5},{14,6},{15,7},{16,24},{17,... | collective-permute-start | bytes 442376 | tf_op jit(solution)/shard_map/ppermute | solution.py:172
  399.8 52.1 %collective-permute-start.40 = (bf16[96,768]{1,0:T(8,128)(2,1)S(1)}, bf16[96,768]{1,0:T(8,128)(2,1)S(1)}, u32[]{:S(2)}, u32[]{:S(2)}) collective-permute-start(bf16[96,768]{1,0:T(8,128)(2,1)S(1)} %broadcast_select_fusion.9), channel_id=1, source_target_pairs={{0,4},{1,5},{2,6},{3,7},{4,0},{5,1},{6,2},{7,3},{8,12},{9,13},{10,... | collective-permute-start | bytes 442376 | tf_op jit(solution)/shard_map/ppermute | solution.py:193
  399.9 67.8 %collective-permute-start.47 = (bf16[96,768]{1,0:T(8,128)(2,1)S(1)}, bf16[96,768]{1,0:T(8,128)(2,1)S(1)}, u32[]{:S(2)}, u32[]{:S(2)}) collective-permute-start(bf16[96,768]{1,0:T(8,128)(2,1)S(1)} %broadcast_select_fusion.8), channel_id=1, source_target_pairs={{0,4},{1,5},{2,6},{3,7},{4,0},{5,1},{6,2},{7,3},{8,12},{9,13},{10,... | collective-permute-start | bytes 442376 | tf_op jit(solution)/shard_map/ppermute | solution.py:193
  403.0 29.0 %collective-permute-start.63 = (bf16[192,3072]{1,0:T(8,128)(2,1)S(1)}, bf16[192,3072]{1,0:T(8,128)(2,1)S(1)}, u32[]{:S(2)}, u32[]{:S(2)}) collective-permute-start(bf16[192,3072]{1,0:T(8,128)(2,1)S(1)} %dynamic-slice_bitcast_fusion.3), channel_id=1, source_target_pairs={{0,2},{1,3},{2,0},{3,1},{4,6},{5,7},{6,4},{7,5},{8,10},{9,11},{10,... | collective-permute-start | bytes 3538952 | tf_op jit(solution)/shard_map/ppermute | solution.py:187
  406.1 69.3 %collective-permute-start.54 = (bf16[96,768]{1,0:T(8,128)(2,1)S(1)}, bf16[96,768]{1,0:T(8,128)(2,1)S(1)}, u32[]{:S(2)}, u32[]{:S(2)}) collective-permute-start(bf16[96,768]{1,0:T(8,128)(2,1)S(1)} %broadcast_select_fusion.7), channel_id=1, source_target_pairs={{0,4},{1,5},{2,6},{3,7},{4,0},{5,1},{6,2},{7,3},{8,12},{9,13},{10,... | collective-permute-start | bytes 442376 | tf_op jit(solution)/shard_map/ppermute | solution.py:193
  406.9 42.5 %collective-permute-start.70 = (bf16[768,768]{1,0:T(8,128)(2,1)S(1)}, bf16[768,768]{1,0:T(8,128)(2,1)S(1)}, u32[]{:S(2)}, u32[]{:S(2)}) collective-permute-start(bf16[768,768]{1,0:T(8,128)(2,1)S(1)} %dynamic-slice_bitcast_fusion.2), channel_id=1, source_target_pairs={{0,2},{1,3},{2,0},{3,1},{4,6},{5,7},{6,4},{7,5},{8,10},{9,11},{10,... | collective-permute-start | bytes 3538952 | tf_op jit(solution)/shard_map/ppermute | solution.py:187
  449.3 53.6 %collective-permute-start.61 = (bf16[96,768]{1,0:T(8,128)(2,1)S(1)}, bf16[96,768]{1,0:T(8,128)(2,1)S(1)}, u32[]{:S(2)}, u32[]{:S(2)}) collective-permute-start(bf16[96,768]{1,0:T(8,128)(2,1)S(1)} %broadcast_select_fusion.6), channel_id=1, source_target_pairs={{0,4},{1,5},{2,6},{3,7},{4,0},{5,1},{6,2},{7,3},{8,12},{9,13},{10,... | collective-permute-start | bytes 442376 | tf_op jit(solution)/shard_map/ppermute | solution.py:193
  474.1 26.3 %collective-permute-start.67 = (bf16[96,3072]{1,0:T(8,128)(2,1)S(1)}, bf16[96,3072]{1,0:T(8,128)(2,1)S(1)}, u32[]{:S(2)}, u32[]{:S(2)}) collective-permute-start(bf16[96,3072]{1,0:T(8,128)(2,1)S(1)} %add_convert_fusion.2), channel_id=1, source_target_pairs={{8,0},{9,1},{10,2},{11,3},{12,4},{13,5},{14,6},{15,7},{16,24},{17,... | collective-permute-start | bytes 1769480 | tf_op jit(solution)/shard_map/ppermute | solution.py:172
  476.4 30.2 %collective-permute-start.74 = (bf16[384,768]{1,0:T(8,128)(2,1)S(1)}, bf16[384,768]{1,0:T(8,128)(2,1)S(1)}, u32[]{:S(2)}, u32[]{:S(2)}) collective-permute-start(bf16[384,768]{1,0:T(8,128)(2,1)S(1)} %add_convert_fusion), channel_id=1, source_target_pairs={{8,0},{9,1},{10,2},{11,3},{12,4},{13,5},{14,6},{15,7},{16,24},{17,... | collective-permute-start | bytes 1769480 | tf_op jit(solution)/shard_map/ppermute | solution.py:172
  (172 other events, 1208.1 us)
